TPU v7x, 256 devices: a whole 4x4x8 slice. The times are simulated.
256 devices in a mesh: ctx: 64 (over x, z_lo, y), dp: 4 (over z_hi, core).
Axes of the slice: x: 4, y: 4, z: 8 (z_hi: 2, z_lo: 4; z = z_hi * 4 + z_lo), core: 2. Of those that a mesh axis runs over, the one named last changes fastest.
Arguments:
- query_in: bfloat16 [256, 131072], P('dp', 'ctx'), may hold values from -6 to 6
- key_in: bfloat16 [256, 131072], P('dp', 'ctx'), may hold values from -6 to 6
- value_in: bfloat16 [256, 131072], P('dp', 'ctx'), may hold values from -6 to 6
- grad_out: bfloat16 [256, 131072], P('dp', 'ctx'), may hold values from -6 to 6
- filter_raw: float32 [64, 131072], P('ctx'), may hold values from -6 to 6
Outputs:
- grad_query: bfloat16 [256, 131072], P('dp', 'ctx')
- grad_key: bfloat16 [256, 131072], P('dp', 'ctx')
- grad_value: bfloat16 [256, 131072], P('dp', 'ctx')
- grad_filter: float32 [64, 131072], P('ctx')
All inputs are finite; a program needn't handle non-finite values.
Results may differ from a plain program's by a relative error of at most 0.015.
Values may be sent and summed in bfloat16 or wider, within the bound.
A program may use at most 128 MiB of HBM per device.

v0:
```python
import math

import jax
import jax.numpy as jnp
from jax import lax
from jax.sharding import PartitionSpec as P

highest = lax.Precision.HIGHEST


def dft_tables(first_len, second_len):
    total_len = first_len * second_len
    half_rows = first_len // 2
    outer = jnp.arange(first_len, dtype=jnp.int32)
    inner = jnp.arange(half_rows, dtype=jnp.int32)
    across = jnp.arange(second_len, dtype=jnp.int32)
    angle_first = (
        2.0
        * math.pi
        / first_len
        * (outer[:, None] * inner[None, :] % first_len).astype(jnp.float32)
    )
    angle_twist = (
        2.0
        * math.pi
        / total_len
        * (outer[:, None] * across[None, :] % total_len).astype(jnp.float32)
    )
    angle_second = (
        2.0
        * math.pi
        / second_len
        * (across[:, None] * across[None, :] % second_len).astype(jnp.float32)
    )
    return (
        jnp.cos(angle_first),
        jnp.sin(angle_first),
        jnp.cos(angle_twist),
        jnp.sin(angle_twist),
        jnp.cos(angle_second),
        jnp.sin(angle_second),
    )


def split_table(table):
    table_high = table.astype(jnp.bfloat16)
    table_rest = (table - table_high.astype(jnp.float32)).astype(jnp.bfloat16)
    return (table_high, table_rest)


def first_section_rows(table, folded_rows):
    table_high, table_rest = split_table(table)
    upper = jnp.einsum("kj,cjb->ckb", table_high, folded_rows, preferred_element_type=jnp.float32)
    lower = jnp.einsum("kj,cjb->ckb", table_rest, folded_rows, preferred_element_type=jnp.float32)
    return upper + lower


def second_section(part_re, part_im, tables):
    cos_first, sin_first, cos_twist, sin_twist, cos_second, sin_second = tables
    twist_re = part_re * cos_twist + part_im * sin_twist
    twist_im = part_im * cos_twist - part_re * sin_twist
    out_re = jnp.einsum("ckj,jb->ckb", twist_re, cos_second, precision=highest) + jnp.einsum(
        "ckj,jb->ckb", twist_im, sin_second, precision=highest
    )
    out_im = jnp.einsum("ckj,jb->ckb", twist_im, cos_second, precision=highest) - jnp.einsum(
        "ckj,jb->ckb", twist_re, sin_second, precision=highest
    )
    return (out_re, out_im)


def spectrum(signal, tables):
    cos_first, sin_first, cos_twist, sin_twist, cos_second, sin_second = tables
    channels = signal.shape[0]
    folded = signal.reshape(channels, cos_first.shape[1], cos_second.shape[0])
    part_re = jnp.einsum("kj,cjb->ckb", cos_first, folded, precision=highest)
    part_im = -jnp.einsum("kj,cjb->ckb", sin_first, folded, precision=highest)
    return second_section(part_re, part_im, tables)


def spectrum_rows(signal, tables):
    cos_first, sin_first, cos_twist, sin_twist, cos_second, sin_second = tables
    channels = signal.shape[0]
    folded = signal.reshape(channels, cos_first.shape[1], cos_second.shape[0])
    part_re = first_section_rows(cos_first, folded)
    part_im = -first_section_rows(sin_first, folded)
    return second_section(part_re, part_im, tables)


def inverse(spec_re, spec_im, tables):
    cos_first, sin_first, cos_twist, sin_twist, cos_second, sin_second = tables
    channels = spec_re.shape[0]
    total_len = cos_first.shape[0] * cos_second.shape[0]
    inner_re = jnp.einsum("ckj,jb->ckb", spec_re, cos_second, precision=highest) - jnp.einsum(
        "ckj,jb->ckb", spec_im, sin_second, precision=highest
    )
    inner_im = jnp.einsum("ckj,jb->ckb", spec_im, cos_second, precision=highest) + jnp.einsum(
        "ckj,jb->ckb", spec_re, sin_second, precision=highest
    )
    twist_re = inner_re * cos_twist - inner_im * sin_twist
    twist_im = inner_im * cos_twist + inner_re * sin_twist
    folded = jnp.einsum("kj,ckb->cjb", cos_first, twist_re, precision=highest) - jnp.einsum(
        "kj,ckb->cjb", sin_first, twist_im, precision=highest
    )
    return folded.reshape(channels, -1) / float(total_len)


def per_device(query_in, key_in, value_in, grad_out, filter_raw):
    gated = (key_in.astype(jnp.float32) * value_in.astype(jnp.float32)).astype(jnp.bfloat16)
    grad_conv = (grad_out.astype(jnp.float32) * query_in.astype(jnp.float32)).astype(jnp.bfloat16)
    gated_chan, grad_chan = (
        lax.all_to_all(gated, "ctx", split_axis=0, concat_axis=1, tiled=True),
        lax.all_to_all(grad_conv, "ctx", split_axis=0, concat_axis=1, tiled=True),
    )
    seq_len = filter_raw.shape[1]
    length_all = 2 * seq_len
    power = length_all.bit_length() - 1
    second_len = 1 << (power - 1) // 2
    first_len = length_all // second_len
    tables = dft_tables(first_len, second_len)
    root = jnp.sqrt(jnp.float32(seq_len))
    filt = filter_raw / root
    filt_re, filt_im = spectrum(filt, tables)
    gated_re, gated_im = spectrum_rows(gated_chan, tables)
    convolved = inverse(
        filt_re * gated_re - filt_im * gated_im, filt_re * gated_im + filt_im * gated_re, tables
    ).astype(jnp.bfloat16)
    grad_re, grad_im = spectrum_rows(grad_chan, tables)
    grad_mixed = inverse(
        filt_re * grad_re + filt_im * grad_im, filt_re * grad_im - filt_im * grad_re, tables
    ).astype(jnp.bfloat16)
    conv_seq, mixed_seq = (
        lax.all_to_all(convolved, "ctx", split_axis=1, concat_axis=0, tiled=True),
        lax.all_to_all(grad_mixed, "ctx", split_axis=1, concat_axis=0, tiled=True),
    )
    cross_re = gated_re * grad_re + gated_im * grad_im
    cross_im = gated_re * grad_im - gated_im * grad_re
    lagged = inverse(cross_re, cross_im, tables)
    grad_filter = lax.psum(lagged.astype(jnp.bfloat16), "dp").astype(jnp.float32) / root
    conv_rows = conv_seq.astype(jnp.float32)
    mixed_rows = mixed_seq.astype(jnp.float32)
    grad_query = (grad_out.astype(jnp.float32) * conv_rows).astype(jnp.bfloat16)
    grad_key = (mixed_rows * value_in.astype(jnp.float32)).astype(jnp.bfloat16)
    grad_value = (mixed_rows * key_in.astype(jnp.float32)).astype(jnp.bfloat16)
    return (grad_query, grad_key, grad_value, grad_filter)


def solution(mesh):
    return jax.shard_map(
        per_device,
        mesh=mesh,
        in_specs=(P("dp", "ctx"), P("dp", "ctx"), P("dp", "ctx"), P("dp", "ctx"), P("ctx", None)),
        out_specs=(P("dp", "ctx"), P("dp", "ctx"), P("dp", "ctx"), P("ctx", None)),
        check_vma=False,
    )
```

profile of v0, /device:TPU:1, one launch (start us, length us, event | category | flops | bytes accessed | tf_op | source)
XLA Modules:
  0.0 397.5 jit_solution(5799137321738116040)
XLA Ops:
  10.5 12.6 %all-to-all-start.2 = ((bf16[64,2,1024]{2,1,0:T(2,128)(2,1)}), bf16[64,2,1024]{2,1,0:T(2,128)(2,1)S(1)}, u32[]{:S(2)}, u32[]{:S(2)}) async-start(bf16[64,2,1024]{2,1,0:T(2,128)(2,1)} %reshape.388), calls=%async_computation.2 | async-start | bytes 524288 | tf_op jit(solution)/shard_map/all_to_all | solution.py:112
  24.7 11.6 %convolution_bitcast_fusion = f32[1,1024,256]{1,2,0:T(8,128)S(1)} fusion(f32[512,256]{1,0:T(8,128)S(1)} %reshape.364), kind=kOutput, calls=%fused_computation.19 | convolution fusion | flops 1617952768 | bytes 1572864 | tf_op jit(solution)/shard_map/kj,cjb->ckb/dot_general | solution.py:75
  36.4 11.9 %fusion.6 = f32[1,1024,256]{1,2,0:T(8,128)S(1)} fusion(f32[512,256]{1,0:T(8,128)S(1)} %reshape.364), kind=kOutput, calls=%fused_computation.18 | convolution fusion | flops 1618214912 | bytes 1572864 | tf_op jit(solution)/shard_map/kj,cjb->ckb/dot_general | solution.py:76
  62.5 7.8 %fusion.44 = f32[1024,256]{1,0:T(8,128)} fusion(f32[1,1024,256]{1,2,0:T(8,128)S(1)} %fusion.6, f32[1,1024,256]{1,2,0:T(8,128)S(1)} %convolution_bitcast_fusion), kind=kOutput, calls=%fused_computation.76 | convolution fusion | flops 810680320 | bytes 3145728 | tf_op jit(solution)/shard_map/ckj,jb->ckb/dot_general | solution.py:62
  72.0 9.5 %convolution_add_fusion.9 = f32[1024,256]{1,0:T(8,128)} fusion(f32[1024,256]{1,0:T(8,128)} %fusion.44, f32[1,1024,256]{1,2,0:T(8,128)S(1)} %convolution_bitcast_fusion, f32[1,1024,256]{1,2,0:T(8,128)} %copy-done.8), kind=kOutput, calls=%fused_computation.41 | convolution fusion | flops 810942464 | bytes 4194304 | tf_op jit(solution)/shard_map/ckj,jb->ckb/dot_general | solution.py:62
  81.6 10.1 %all-to-all-start = ((bf16[64,2,1024]{2,1,0:T(2,128)(2,1)}), bf16[64,2,1024]{2,1,0:T(2,128)(2,1)S(1)}, u32[]{:S(2)}, u32[]{:S(2)}) async-start(bf16[64,2,1024]{2,1,0:T(2,128)(2,1)} %reshape.384), calls=%async_computation | async-start | bytes 524288 | tf_op jit(solution)/shard_map/all_to_all | solution.py:111
  93.6 10.1 %fusion.87 = f32[256,1024]{1,0:T(8,128)} fusion(bf16[512,256]{1,0:T(8,128)(2,1)S(1)} %reshape.370), kind=kOutput, calls=%fused_computation.121 | convolution fusion | flops 276299776 | bytes 1310720 | tf_op jit(solution)/shard_map/kj,cjb->ckb/dot_general | solution.py:53
  103.7 10.1 %fusion.83 = f32[256,1024]{1,0:T(8,128)} fusion(bf16[512,256]{1,0:T(8,128)(2,1)S(1)} %reshape.370), kind=kOutput, calls=%fused_computation.119 | convolution fusion | flops 276299776 | bytes 1310720 | tf_op jit(solution)/shard_map/kj,cjb->ckb/dot_general | solution.py:53
  115.6 8.8 %fusion.85 = f32[256,1024]{1,0:T(8,128)S(1)} fusion(bf16[512,256]{1,0:T(8,128)(2,1)S(1)} %reshape.367), kind=kOutput, calls=%fused_computation.120 | convolution fusion | flops 276299776 | bytes 1310720 | tf_op jit(solution)/shard_map/kj,cjb->ckb/dot_general | solution.py:53
  124.5 8.7 %fusion.89 = f32[256,1024]{1,0:T(8,128)S(1)} fusion(bf16[512,256]{1,0:T(8,128)(2,1)S(1)} %reshape.367), kind=kOutput, calls=%fused_computation.122 | convolution fusion | flops 276299776 | bytes 1310720 | tf_op jit(solution)/shard_map/kj,cjb->ckb/dot_general | solution.py:53
  133.2 9.5 %fusion.9 = f32[1,1024,256]{1,2,0:T(8,128)S(1)} fusion(f32[256,1024]{1,0:T(8,128)S(1)} %copy-done.9, bf16[512,256]{1,0:T(8,128)(2,1)S(1)} %reshape.370), kind=kOutput, calls=%fused_computation.30 | convolution fusion | flops 278134784 | bytes 2359296 | tf_op jit(solution)/shard_map/kj,cjb->ckb/dot_general | solution.py:54
  142.7 9.3 %fusion.8 = f32[1,1024,256]{1,2,0:T(8,128)S(1)} fusion(f32[256,1024]{1,0:T(8,128)S(1)} %copy-done.10, bf16[512,256]{1,0:T(8,128)(2,1)S(1)} %reshape.370), kind=kOutput, calls=%fused_computation.28 | convolution fusion | flops 278396928 | bytes 2359296 | tf_op jit(solution)/shard_map/kj,cjb->ckb/dot_general | solution.py:54
  165.8 9.4 %fusion.11 = f32[1,1024,256]{1,2,0:T(8,128)S(1)} fusion(f32[256,1024]{1,0:T(8,128)S(1)} %fusion.85, bf16[512,256]{1,0:T(8,128)(2,1)S(1)} %reshape.367), kind=kOutput, calls=%fused_computation.38 | convolution fusion | flops 278396928 | bytes 2359296 | tf_op jit(solution)/shard_map/kj,cjb->ckb/dot_general | solution.py:54
  175.2 9.1 %fusion.12 = f32[1,1024,256]{1,2,0:T(8,128)S(1)} fusion(f32[256,1024]{1,0:T(8,128)S(1)} %fusion.89, bf16[512,256]{1,0:T(8,128)(2,1)S(1)} %reshape.367), kind=kOutput, calls=%fused_computation.40 | convolution fusion | flops 278134784 | bytes 2359296 | tf_op jit(solution)/shard_map/kj,cjb->ckb/dot_general | solution.py:54
  219.0 7.6 %multiply_add_fusion = (f32[1024,256]{1,0:T(8,128)S(1)}, f32[1024,256]{1,0:T(8,128)S(1)}, f32[1024,256]{1,0:T(8,128)S(1)}, f32[1024,256]{1,0:T(8,128)S(1)}, f32[1024,256]{1,0:T(8,128)S(1)}, /*index=5*/f32[1024,256]{1,0:T(8,128)S(1)}) fusion(f32[1024,256]{1,0:T(8,128)S(1)} %convolution_subtract_fusion.2, f32[1024,256]{1,0:T(8,128)S(1)} %convolution_add_fusion.6, ...), kind=kOutput, calls=%fused_computation.86 | convolution fusion | flops 815661056 | bytes 14680064 | tf_op jit(solution)/shard_map/ckj,jb->ckb/dot_general | solution.py:65
  245.0 14.1 %fusion.63 = f32[256,512]{1,0:T(8,128)S(1)} fusion(f32[1024,256]{1,0:T(8,128)S(1)} %convolution_add_fusion.5, f32[1024,256]{1,0:T(8,128)S(1)} %convolution_subtract_fusion.3), kind=kOutput, calls=%fused_computation.101 | convolution fusion | flops 1622409216 | bytes 2621440 | tf_op jit(solution)/shard_map/kj,ckb->cjb/dot_general | solution.py:101
  259.0 14.1 %fusion.21 = bf16[1,512,256]{1,2,0:T(8,128)(2,1)S(1)} fusion(f32[256,512]{1,0:T(8,128)S(1)} %fusion.63, f32[1024,256]{1,0:T(8,128)S(1)} %convolution_subtract_fusion.3, f32[1024,256]{1,0:T(8,128)S(1)} %convolution_add_fusion.5), kind=kOutput, calls=%fused_computation.53 | convolution fusion | flops 1622802432 | bytes 2883584 | tf_op jit(solution)/shard_map/kj,ckb->cjb/dot_general | solution.py:101
  276.5 10.1 %all-to-all-start.1 = ((bf16[64,2,1024]{2,1,0:T(2,128)(2,1)}), bf16[64,2,1024]{2,1,0:T(2,128)(2,1)S(1)}, u32[]{:S(2)}, u32[]{:S(2)}) async-start(bf16[64,2,1024]{2,1,0:T(2,128)(2,1)} %reshape.386), calls=%async_computation.1 | async-start | bytes 524288 | tf_op jit(solution)/shard_map/all_to_all | solution.py:132
  294.7 13.9 %fusion.49 = f32[256,512]{1,0:T(8,128)S(1)} fusion(f32[1024,256]{1,0:T(8,128)S(1)} %convolution_add_fusion, f32[1024,256]{1,0:T(8,128)S(1)} %convolution_subtract_fusion), kind=kOutput, calls=%fused_computation.81 | convolution fusion | flops 1622409216 | bytes 2621440 | tf_op jit(solution)/shard_map/kj,ckb->cjb/dot_general | solution.py:101
  308.6 14.3 %fusion.19 = bf16[1,512,256]{1,2,0:T(8,128)(2,1)S(1)} fusion(f32[256,512]{1,0:T(8,128)S(1)} %fusion.49, f32[1024,256]{1,0:T(8,128)S(1)} %convolution_subtract_fusion, f32[1024,256]{1,0:T(8,128)S(1)} %convolution_add_fusion), kind=kOutput, calls=%fused_computation.51 | convolution fusion | flops 1622802432 | bytes 2883584 | tf_op jit(solution)/shard_map/kj,ckb->cjb/dot_general | solution.py:101
  324.4 13.9 %fusion.56 = f32[256,512]{1,0:T(8,128)S(1)} fusion(f32[1024,256]{1,0:T(8,128)S(1)} %copy-done.1, f32[1024,256]{1,0:T(8,128)S(1)} %copy-done.2), kind=kOutput, calls=%fused_computation.90 | convolution fusion | flops 1622409216 | bytes 2621440 | tf_op jit(solution)/shard_map/kj,ckb->cjb/dot_general | solution.py:101
  338.2 14.0 %fusion.20 = bf16[1,512,256]{1,2,0:T(8,128)(2,1)S(1)} fusion(f32[256,512]{1,0:T(8,128)S(1)} %fusion.56, f32[1024,256]{1,0:T(8,128)S(1)} %copy-done.2, f32[1024,256]{1,0:T(8,128)S(1)} %copy-done.1), kind=kOutput, calls=%fused_computation.52 | convolution fusion | flops 1622802432 | bytes 2883584 | tf_op jit(solution)/shard_map/kj,ckb->cjb/dot_general | solution.py:101
  355.6 10.1 %all-to-all-start.3 = ((bf16[64,2,1024]{2,1,0:T(2,128)(2,1)}), bf16[64,2,1024]{2,1,0:T(2,128)(2,1)S(1)}, u32[]{:S(2)}, u32[]{:S(2)}) async-start(bf16[64,2,1024]{2,1,0:T(2,128)(2,1)} %reshape.390), calls=%async_computation.3 | async-start | bytes 524288 | tf_op jit(solution)/shard_map/all_to_all | solution.py:133
  365.7 19.5 %all-reduce.2.cloned.1.call-done = bf16[1,131072]{1,0:T(2,128)(2,1)} async-done(((bf16[1,131072]{1,0:T(2,128)(2,1)}), bf16[1,131072]{1,0:T(2,128)(2,1)}) %all-reduce.2.cloned.1.call-update) | async-done | bytes 262160 | tf_op jit(solution)/shard_map/psum | solution.py:138
  (79 shorter events, 112.3 us)
Async XLA Ops:
  7.2 15.9 %copy-start.7 = (f32[1,131072]{1,0:T(1,128)S(1)}, f32[1,131072]{1,0:T(1,128)}, u32[]{:S(2)}) copy-start(f32[1,131072]{1,0:T(1,128)} %param.9) | copy-start | bytes 1572868
  10.5 71.1 %all-to-all-start.2 = ((bf16[64,2,1024]{2,1,0:T(2,128)(2,1)}), bf16[64,2,1024]{2,1,0:T(2,128)(2,1)S(1)}, u32[]{:S(2)}, u32[]{:S(2)}) async-start(bf16[64,2,1024]{2,1,0:T(2,128)(2,1)} %reshape.388), calls=%async_computation.2 | async-start | bytes 524288 | tf_op jit(solution)/shard_map/all_to_all | solution.py:112
  48.3 14.2 %copy-start.8 = (f32[1,1024,256]{1,2,0:T(8,128)}, f32[1,1024,256]{1,2,0:T(8,128)S(1)}, u32[]{:S(2)}) copy-start(f32[1,1024,256]{1,2,0:T(8,128)S(1)} %fusion.6) | copy-start | bytes 3145732
  55.1 7.3 %copy-start.3 = (bf16[64,2048]{1,0:T(8,128)(2,1)S(1)}, bf16[64,2048]{1,0:T(8,128)(2,1)}, u32[]{:S(2)}) copy-start(bf16[64,2048]{1,0:T(8,128)(2,1)} %param.6) | copy-start | bytes 786436
  55.1 7.3 %copy-start.5 = (bf16[64,2048]{1,0:T(8,128)(2,1)S(1)}, bf16[64,2048]{1,0:T(8,128)(2,1)}, u32[]{:S(2)}) copy-start(bf16[64,2048]{1,0:T(8,128)(2,1)} %param.7) | copy-start | bytes 786436
  81.6 32.2 %all-to-all-start = ((bf16[64,2,1024]{2,1,0:T(2,128)(2,1)}), bf16[64,2,1024]{2,1,0:T(2,128)(2,1)S(1)}, u32[]{:S(2)}, u32[]{:S(2)}) async-start(bf16[64,2,1024]{2,1,0:T(2,128)(2,1)} %reshape.384), calls=%async_computation | async-start | bytes 524288 | tf_op jit(solution)/shard_map/all_to_all | solution.py:111
  124.4 8.7 %copy-start.9 = (f32[256,1024]{1,0:T(8,128)S(1)}, f32[256,1024]{1,0:T(8,128)}, u32[]{:S(2)}) copy-start(f32[256,1024]{1,0:T(8,128)} %fusion.87) | copy-start | bytes 3145732
  133.2 9.5 %copy-start.10 = (f32[256,1024]{1,0:T(8,128)S(1)}, f32[256,1024]{1,0:T(8,128)}, u32[]{:S(2)}) copy-start(f32[256,1024]{1,0:T(8,128)} %fusion.83) | copy-start | bytes 3145732
  212.2 6.9 %copy-start = (f32[1024,256]{1,0:T(8,128)S(1)}, f32[1024,256]{1,0:T(8,128)}, u32[]{:S(2)}) copy-start(f32[1024,256]{1,0:T(8,128)} %convolution_add_fusion.9) | copy-start | bytes 3145732
  276.5 79.1 %all-to-all-start.1 = ((bf16[64,2,1024]{2,1,0:T(2,128)(2,1)}), bf16[64,2,1024]{2,1,0:T(2,128)(2,1)S(1)}, u32[]{:S(2)}, u32[]{:S(2)}) async-start(bf16[64,2,1024]{2,1,0:T(2,128)(2,1)} %reshape.386), calls=%async_computation.1 | async-start | bytes 524288 | tf_op jit(solution)/shard_map/all_to_all | solution.py:132
  286.6 98.6 %all-reduce.2.cloned.1.call-start = ((), (), s32[]{:S(2)}) async-start(), calls=%async_computation.4 | async-start | bytes 1048576 | tf_op jit(solution)/shard_map/psum | solution.py:138
  308.6 15.7 %copy-start.2 = (f32[1024,256]{1,0:T(8,128)S(1)}, f32[1024,256]{1,0:T(8,128)}, u32[]{:S(2)}) copy-start(f32[1024,256]{1,0:T(8,128)} %convolution_subtract_fusion.1) | copy-start | bytes 3145732
  323.0 1.4 copy-start.1
  355.6 33.0 %all-to-all-start.3 = ((bf16[64,2,1024]{2,1,0:T(2,128)(2,1)}), bf16[64,2,1024]{2,1,0:T(2,128)(2,1)S(1)}, u32[]{:S(2)}, u32[]{:S(2)}) async-start(bf16[64,2,1024]{2,1,0:T(2,128)(2,1)} %reshape.390), calls=%async_computation.3 | async-start | bytes 524288 | tf_op jit(solution)/shard_map/all_to_all | solution.py:133
  388.0 1.0 copy-start.4
  388.0 1.0 copy-start.6
Sparse Core Ops, SparseCore 0:
  324.5 60.6 all-reduce.1
where the time goes:
time: 405 us; the launch traced here: 397 us
  matrix products  296 us (73%)
  starting transfers between devices  43.1 us (11%)
  waiting for transfers between devices  19.5 us (5%)
  other arithmetic  15.9 us (4%)
  between operations  15.1 us (4%)
  local copies, waits for them, and re-layouts  7.49 us (2%)
    dot_general x3, matrix products, inverse(): jnp.einsum('kj,ckb->cjb', sin_first, twist_im, precision=highest)  42.5 us
    dot_general x3, matrix products, inverse(): jnp.einsum('kj,ckb->cjb', cos_first, twist_re, precision=highest)  41.8 us
    dot_general x4, matrix products, first_section_rows(): jnp.einsum('kj,cjb->ckb', table_high, folded_rows, preferred_element_type...  37.7 us
    dot_general x4, matrix products, first_section_rows(): jnp.einsum('kj,cjb->ckb', table_rest, folded_rows, preferred_element_type...  37.2 us
    dot_general x3, matrix products, second_section(): jnp.einsum('ckj,jb->ckb', twist_im, sin_second, precision=highest)  23.4 us
    dot_general x3, matrix products, second_section(): jnp.einsum('ckj,jb->ckb', twist_re, sin_second, precision=highest)  21.7 us
    dot_general x3, matrix products, second_section(): jnp.einsum('ckj,jb->ckb', twist_re, cos_second, precision=highest)  21.6 us
    dot_general x3, matrix products, second_section(): jnp.einsum('ckj,jb->ckb', twist_im, cos_second, precision=highest)  20.8 us
  transfers between devices with their start and end apart: 5, of which 1 were waited for; matrix products, arithmetic and copies ran while one was open for 38% of the time, Pallas kernels for 0%

commit v1 on v0

v1 whole, which is shorter than its diff:
```python
import functools
import math

import jax
import jax.numpy as jnp
import numpy as np
from jax import lax
from jax.experimental import pallas as pl
from jax.experimental.pallas import tpu as pltpu
from jax.sharding import PartitionSpec as P

LANES = 128
ACROSS = 256
PIECE = 2048
ROWS = PIECE // ACROSS

f32 = jnp.float32
bf16 = jnp.bfloat16


def make_tables(half_rows):
    total = 2 * half_rows * ACROSS
    freq = np.arange(half_rows)[:, None]
    row = np.arange(half_rows)[None, :]
    across = np.arange(ACROSS)
    angle = (row * (2 * freq + 1)) % (4 * half_rows) * (2 * math.pi / (4 * half_rows))
    chunk = half_rows // 2
    cos, sin = np.cos(angle), np.sin(angle)
    first = np.concatenate([cos[:chunk], -sin[:chunk], cos[chunk:], -sin[chunk:]], 0)
    last = np.concatenate([cos, -sin], 0).T
    twist = across[None, :] * (2 * freq + 1) * (2 * math.pi / (2 * total))
    inner = (across[:, None] * across[None, :]) % ACROSS * (2 * math.pi / ACROSS)
    re, im = np.cos(inner), -np.sin(inner)
    second = np.block([[re, im], [-im, re]])
    back = np.block([[re, -im], [im, re]])
    narrow = [t.astype(np.float32).astype(bf16) for t in (first, last, second, back)]
    return narrow + [np.cos(twist).astype(np.float32), -np.sin(twist).astype(np.float32)]


def kernel(
    parts,
    q_ref, k_ref, v_ref, go_ref, h_ref,
    first_hbm, last_hbm, second_hbm, back_hbm, tre_hbm, tim_hbm,
    gq_ref, gk_ref, gv_ref, gf_ref,
    first_ref, last_ref, second_ref, back_ref, tre_ref, tim_ref,
    turn_ref, msg_x, msg_g, msg_c, msg_m, got_x, got_g, got_c, got_m,
    signal_ref, mid_ref, spec_h, spec_x, spec_g,
    lag_ref, lag_in, pair_ref, pair_in, total_ref,
    table_sem, send_sem, recv_sem, pair_send, pair_recv,
):
    half_rows = parts * ROWS
    seq = half_rows * ACROSS
    me = lax.axis_index("ctx")
    group = lax.axis_index("dp")
    core = lax.rem(group, 2)
    high = group // 2
    other_core = high * 2 + (1 - core)
    other_high = (1 - high) * 2 + core
    MESH = pl.DeviceIdType.MESH

    barrier = pltpu.get_barrier_semaphore()

    def greet(step, carry):
        pl.semaphore_signal(
            barrier, inc=1, device_id=(lax.rem(me + step, parts), group), device_id_type=MESH
        )
        return carry

    lax.fori_loop(1, parts, greet, 0)
    pl.semaphore_signal(barrier, inc=1, device_id=(me, other_core), device_id_type=MESH)
    pl.semaphore_signal(barrier, inc=1, device_id=(me, other_high), device_id_type=MESH)

    table_copies = [
        pltpu.make_async_copy(src, dst, table_sem.at[i])
        for i, (src, dst) in enumerate(
            (
                (first_hbm, first_ref),
                (tre_hbm, tre_ref),
                (tim_hbm, tim_ref),
                (second_hbm, second_ref),
                (back_hbm, back_ref),
                (last_hbm, last_ref),
            )
        )
    ]
    for copy in table_copies:
        copy.start()

    def gate(a_ref, b_ref, msg_ref):
        for j in range(PIECE // LANES):
            cols = slice(j * LANES, (j + 1) * LANES)
            slot = (j % 2) * ROWS + j // 2
            turn_ref[pl.ds(slot, parts, stride=16), :] = a_ref[:, cols].astype(f32) * b_ref[
                :, cols
            ].astype(f32)
        msg_ref[...] = turn_ref[...].reshape(parts, 16, LANES).astype(bf16)

    def send_all(msg_ref, got_ref, which):
        def send(step, carry):
            to = lax.rem(me + step, parts)
            pltpu.make_async_remote_copy(
                src_ref=msg_ref.at[to],
                dst_ref=got_ref.at[me],
                send_sem=send_sem.at[which],
                recv_sem=recv_sem.at[which],
                device_id=(to, group),
                device_id_type=MESH,
            ).start()
            return carry

        lax.fori_loop(1, parts, send, 0)
        got_ref[me] = msg_ref[me]

    def whole(ref, sem):
        return pltpu.make_async_copy(
            ref.at[pl.ds(0, parts - 1)], ref.at[pl.ds(0, parts - 1)], sem
        )

    def unfold(got_ref):
        got = got_ref[...].astype(f32)
        for half in range(2):
            signal_ref[:, half * LANES : (half + 1) * LANES] = (
                got[:, half * ROWS : (half + 1) * ROWS, :].reshape(half_rows, LANES).astype(bf16)
            )

    chunk = half_rows // 2

    def forward(spec_ref):
        def body(c, carry):
            rows = pl.ds(pl.multiple_of(c * chunk, chunk), chunk)
            both = jnp.dot(
                first_ref[pl.ds(pl.multiple_of(c * 2 * chunk, 2 * chunk), 2 * chunk), :],
                signal_ref[...],
                preferred_element_type=f32,
            )
            re, im = both[:chunk], both[chunk:]
            tre, tim = tre_ref[rows, :], tim_ref[rows, :]
            turned = jnp.concatenate([re * tre - im * tim, re * tim + im * tre], 1).astype(bf16)
            spec_ref[rows, :] = jnp.dot(turned, second_ref[...], preferred_element_type=f32)
            return carry

        lax.fori_loop(0, 2, body, 0)

    def inverse_mid(a_spec, b_spec, conj):
        def body(c, carry):
            rows = pl.ds(pl.multiple_of(c * chunk, chunk), chunk)
            a_re, a_im = a_spec[rows, :ACROSS], a_spec[rows, ACROSS:]
            b_re, b_im = b_spec[rows, :ACROSS], b_spec[rows, ACROSS:]
            if conj:
                re, im = a_re * b_re + a_im * b_im, a_re * b_im - a_im * b_re
            else:
                re, im = a_re * b_re - a_im * b_im, a_re * b_im + a_im * b_re
            inner = jnp.dot(
                jnp.concatenate([re, im], 1).astype(bf16), back_ref[...], preferred_element_type=f32
            )
            re, im = inner[:, :ACROSS], inner[:, ACROSS:]
            tre, tim = tre_ref[rows, :], tim_ref[rows, :]
            mid_ref[rows, :] = (re * tre + im * tim).astype(bf16)
            mid_ref[pl.ds(pl.multiple_of(half_rows + c * chunk, chunk), chunk), :] = (
                im * tre - re * tim
            ).astype(bf16)
            return carry

        lax.fori_loop(0, 2, body, 0)

    def inverse_rows(c, scale):
        rows = pl.ds(pl.multiple_of(c * chunk, chunk), chunk)
        return (
            jnp.dot(last_ref[rows, :], mid_ref[...], preferred_element_type=f32) * scale
        )

    def inverse_to_msg(a_spec, b_spec, conj, msg_ref):
        inverse_mid(a_spec, b_spec, conj)

        def body(c, carry):
            out = inverse_rows(c, 1.0 / seq)
            out = jnp.concatenate(
                [
                    out[:, :LANES].reshape(parts // 2, ROWS, LANES),
                    out[:, LANES:].reshape(parts // 2, ROWS, LANES),
                ],
                1,
            )
            msg_ref[pl.ds(c * (parts // 2), parts // 2)] = out.astype(bf16)
            return carry

        lax.fori_loop(0, 2, body, 0)

    gate(k_ref, v_ref, msg_x)
    pl.semaphore_wait(barrier, parts + 1)
    send_all(msg_x, got_x, 0)
    gate(go_ref, q_ref, msg_g)
    send_all(msg_g, got_g, 1)

    root = math.sqrt(seq)
    for half in range(2):
        signal_ref[:, half * LANES : (half + 1) * LANES] = (
            h_ref[pl.ds(half, half_rows, stride=2), :] * (1.0 / root)
        ).astype(bf16)
    for copy in table_copies[:4]:
        copy.wait()
    forward(spec_h)

    whole(got_x, recv_sem.at[0]).wait()
    unfold(got_x)
    forward(spec_x)
    for copy in table_copies[4:]:
        copy.wait()
    inverse_to_msg(spec_h, spec_x, False, msg_c)
    send_all(msg_c, got_c, 2)

    whole(got_g, recv_sem.at[1]).wait()
    unfold(got_g)
    forward(spec_g)

    inverse_mid(spec_x, spec_g, True)

    def lag_body(c, carry):
        lag_ref[c] = inverse_rows(c, 1.0 / (seq * root)).astype(bf16)
        return carry

    lax.fori_loop(0, 2, lag_body, 0)

    to_core = pltpu.make_async_remote_copy(
        src_ref=lag_ref.at[1 - core],
        dst_ref=lag_in,
        send_sem=pair_send.at[0],
        recv_sem=pair_recv.at[0],
        device_id=(me, other_core),
        device_id_type=MESH,
    )
    to_core.start()

    inverse_to_msg(spec_h, spec_g, True, msg_m)
    to_core.wait_recv()
    pair_ref[...] = (lag_ref[core].astype(f32) + lag_in[...].astype(f32)).astype(bf16)
    to_high = pltpu.make_async_remote_copy(
        src_ref=pair_ref,
        dst_ref=pair_in,
        send_sem=pair_send.at[1],
        recv_sem=pair_recv.at[1],
        device_id=(me, other_high),
        device_id_type=MESH,
    )
    to_high.start()
    send_all(msg_m, got_m, 3)

    whole(got_c, recv_sem.at[2]).wait()
    turn_ref[...] = got_c[...].astype(f32).reshape(parts * 16, LANES)
    for j in range(PIECE // LANES):
        cols = slice(j * LANES, (j + 1) * LANES)
        slot = (j % 2) * ROWS + j // 2
        conv = turn_ref[pl.ds(slot, parts, stride=16), :]
        gq_ref[:, cols] = (go_ref[:, cols].astype(f32) * conv).astype(bf16)

    to_high.wait_recv()
    total_ref[core] = pair_ref[...].astype(f32) + pair_in[...].astype(f32)
    to_core_again = pltpu.make_async_remote_copy(
        src_ref=total_ref.at[core],
        dst_ref=total_ref.at[core],
        send_sem=pair_send.at[2],
        recv_sem=pair_recv.at[2],
        device_id=(me, other_core),
        device_id_type=MESH,
    )
    to_core_again.start()

    whole(got_m, recv_sem.at[3]).wait()
    turn_ref[...] = got_m[...].astype(f32).reshape(parts * 16, LANES)
    for j in range(PIECE // LANES):
        cols = slice(j * LANES, (j + 1) * LANES)
        slot = (j % 2) * ROWS + j // 2
        mixed = turn_ref[pl.ds(slot, parts, stride=16), :]
        gk_ref[:, cols] = (mixed * v_ref[:, cols].astype(f32)).astype(bf16)
        gv_ref[:, cols] = (mixed * k_ref[:, cols].astype(f32)).astype(bf16)

    to_core_again.wait_recv()
    for c in range(2):
        for half in range(2):
            gf_ref[pl.ds(c * half_rows + half, chunk, stride=2), :] = total_ref[
                c, :, half * LANES : (half + 1) * LANES
            ]
    for which, ref in enumerate((msg_x, msg_g, msg_c, msg_m)):
        whole(ref, send_sem.at[which]).wait()
    to_core.wait_send()
    to_high.wait_send()
    to_core_again.wait_send()


def per_device(parts, query_in, key_in, value_in, grad_out, filter_raw):
    half_rows = parts * ROWS
    seq = half_rows * ACROSS
    tables = make_tables(half_rows)
    vmem = pl.BlockSpec(memory_space=pltpu.VMEM)
    anywhere = pl.BlockSpec(memory_space=pl.ANY)
    window = jax.ShapeDtypeStruct((parts, PIECE), bf16)
    message = pltpu.VMEM((parts, 16, LANES), bf16)
    spectrum = pltpu.VMEM((half_rows, 2 * ACROSS), f32)
    half = (half_rows // 2, ACROSS)
    outs = pl.pallas_call(
        functools.partial(kernel, parts),
        out_shape=(window, window, window, jax.ShapeDtypeStruct((seq // LANES, LANES), f32)),
        in_specs=[vmem] * 5 + [anywhere] * 6,
        out_specs=(vmem, vmem, vmem, vmem),
        scratch_shapes=[pltpu.VMEM(t.shape, t.dtype) for t in tables]
        + [pltpu.VMEM((parts * 16, LANES), f32)]
        + [message] * 8
        + [
            pltpu.VMEM((half_rows, ACROSS), bf16),
            pltpu.VMEM((2 * half_rows, ACROSS), bf16),
            spectrum,
            spectrum,
            spectrum,
            pltpu.VMEM((2,) + half, bf16),
            pltpu.VMEM(half, bf16),
            pltpu.VMEM(half, bf16),
            pltpu.VMEM(half, bf16),
            pltpu.VMEM((2,) + half, f32),
            pltpu.SemaphoreType.DMA((6,)),
            pltpu.SemaphoreType.DMA((4,)),
            pltpu.SemaphoreType.DMA((4,)),
            pltpu.SemaphoreType.DMA((3,)),
            pltpu.SemaphoreType.DMA((3,)),
        ],
        compiler_params=pltpu.CompilerParams(
            collective_id=0, has_side_effects=True, vmem_limit_bytes=48 * 1024 * 1024
        ),
        name="gated_conv_backward",
    )(
        query_in,
        key_in,
        value_in,
        grad_out,
        filter_raw.reshape(seq // LANES, LANES),
        *(jnp.asarray(t) for t in tables),
    )
    return (outs[0], outs[1], outs[2], outs[3].reshape(1, seq))


def solution(mesh):
    return jax.shard_map(
        functools.partial(per_device, mesh.shape["ctx"]),
        mesh=mesh,
        in_specs=(P("dp", "ctx"), P("dp", "ctx"), P("dp", "ctx"), P("dp", "ctx"), P("ctx", None)),
        out_specs=(P("dp", "ctx"), P("dp", "ctx"), P("dp", "ctx"), P("ctx", None)),
        check_vma=False,
    )
```

time: 405 us -> 58.1 us (0.14); the launches traced: 397 us -> 57 us
  matrix products: 296 us -> 0 us
  Pallas kernels: 0 us -> 43.2 us
  starting transfers between devices: 43.1 us -> 0 us
  waiting for transfers between devices: 19.5 us -> 0 us
  other arithmetic: 15.9 us -> 0 us
  between operations: 15.1 us -> 0.66 us
  local copies, waits for them, and re-layouts: 7.49 us -> 13.1 us
    dot_general x40 -> x0, matrix products: 296 us -> none  [the longest x3 42.5 us: inverse(): jnp.einsum('kj,ckb->cjb', sin_first, twist_im, precision=highest)]
    pallas_call x0 -> x1, Pallas kernels: none -> 43.2 us  [per_device(): pl.pallas_call(functools.partial(kernel, parts), out_shape=(window, windo...]
    all_to_all x4 -> x0, starting transfers between devices: 42.9 us -> none  [the longest x1 12.6 us: per_device(): lax.all_to_all(grad_conv, 'ctx', split_axis=0, concat_axis=1, tiled=True)]
    psum x1 -> x0, waiting for transfers between devices: 19.5 us -> none  [per_device(): lax.psum(lagged.astype(jnp.bfloat16), 'dp').astype(jnp.float32) / root]
    unnamed x31 -> x24, local copies, waits for them, and re-layouts: 5.9 us -> 13.1 us
    all_to_all x6 -> x0, other arithmetic: 5.78 us -> none  [the longest x3 3.43 us: per_device(): lax.all_to_all(grad_conv, 'ctx', split_axis=0, concat_axis=1, tiled=True)]
    unnamed x2 -> x0, other arithmetic: 4.31 us -> none
    div x2 -> x0, other arithmetic: 4.05 us -> none  [the longest x1 2.55 us: per_device(): lax.psum(lagged.astype(jnp.bfloat16), 'dp').astype(jnp.float32) / root]
  transfers between devices with their start and end apart: 5 -> 0, of which waited for: 1 -> 0; matrix products, arithmetic and copies ran while one was open for 38% -> 0% of each run, Pallas kernels for 0% -> 0%
where the time goes in v1:
time: 58.1 us; the launch traced here: 57 us
  Pallas kernels  43.2 us (74%)
  local copies, waits for them, and re-layouts  13.1 us (23%)
  between operations  0.66 us (1%)
    pallas_call x1, Pallas kernels, per_device(): pl.pallas_call(functools.partial(kernel, parts), out_shape=(window, windo...  43.2 us
    unnamed x24, local copies, waits for them, and re-layouts  13.1 us

profile of v1, /device:TPU:1, one launch (start us, length us, event | category | flops | bytes accessed | tf_op | source)
XLA Modules:
  0.0 57.0 jit_solution(4768373771416504305)
XLA Ops:
  0.6 0.0 copy-start
  0.6 1.2 %copy-done = bf16[1024,512]{1,0:T(8,128)(2,1)S(1)} copy-done((bf16[1024,512]{1,0:T(8,128)(2,1)S(1)}, bf16[1024,512]{1,0:T(8,128)(2,1)}, u32[]{:S(2)}) %copy-start) | copy-done | bytes 1048600
  1.9 0.0 copy-start.1
  1.9 1.0 %copy-done.1 = f32[1,131072]{1,0:T(1,128)S(1)} copy-done((f32[1,131072]{1,0:T(1,128)S(1)}, f32[1,131072]{1,0:T(1,128)}, u32[]{:S(2)}) %copy-start.1) | copy-done | bytes 524312
  2.9 0.0 copy-start.2
  2.9 1.0 %copy-done.2 = f32[512,256]{1,0:T(8,128)S(1)} copy-done((f32[512,256]{1,0:T(8,128)S(1)}, f32[512,256]{1,0:T(8,128)}, u32[]{:S(2)}) %copy-start.2) | copy-done | bytes 524312
  3.9 0.0 copy-start.3
  3.9 1.0 %copy-done.3 = f32[512,256]{1,0:T(8,128)S(1)} copy-done((f32[512,256]{1,0:T(8,128)S(1)}, f32[512,256]{1,0:T(8,128)}, u32[]{:S(2)}) %copy-start.3) | copy-done | bytes 524312
  5.0 0.0 copy-start.4
  5.0 1.0 %copy-done.4 = bf16[512,512]{1,0:T(8,128)(2,1)S(1)} copy-done((bf16[512,512]{1,0:T(8,128)(2,1)S(1)}, bf16[512,512]{1,0:T(8,128)(2,1)}, u32[]{:S(2)}) %copy-start.4) | copy-done | bytes 524312
  6.0 0.0 copy-start.5
  6.0 1.0 %copy-done.5 = bf16[512,512]{1,0:T(8,128)(2,1)S(1)} copy-done((bf16[512,512]{1,0:T(8,128)(2,1)S(1)}, bf16[512,512]{1,0:T(8,128)(2,1)}, u32[]{:S(2)}) %copy-start.5) | copy-done | bytes 524312
  7.1 0.0 copy-start.6
  7.1 0.9 %copy-done.6 = bf16[64,2048]{1,0:T(8,128)(2,1)S(1)} copy-done((bf16[64,2048]{1,0:T(8,128)(2,1)S(1)}, bf16[64,2048]{1,0:T(8,128)(2,1)}, u32[]{:S(2)}) %copy-start.6) | copy-done | bytes 262168
  8.0 0.0 copy-start.7
  8.0 0.9 %copy-done.7 = bf16[64,2048]{1,0:T(8,128)(2,1)S(1)} copy-done((bf16[64,2048]{1,0:T(8,128)(2,1)S(1)}, bf16[64,2048]{1,0:T(8,128)(2,1)}, u32[]{:S(2)}) %copy-start.7) | copy-done | bytes 262168
  9.0 0.0 copy-start.8
  9.0 0.9 %copy-done.8 = bf16[64,2048]{1,0:T(8,128)(2,1)S(1)} copy-done((bf16[64,2048]{1,0:T(8,128)(2,1)S(1)}, bf16[64,2048]{1,0:T(8,128)(2,1)}, u32[]{:S(2)}) %copy-start.8) | copy-done | bytes 262168
  9.9 0.9 %copy-done.9 = bf16[64,2048]{1,0:T(8,128)(2,1)S(1)} copy-done((bf16[64,2048]{1,0:T(8,128)(2,1)S(1)}, bf16[64,2048]{1,0:T(8,128)(2,1)}, u32[]{:S(2)}) %copy-start.9) | copy-done | bytes 262168
  10.9 43.2 %gated_conv_backward.1 = (bf16[64,2048]{1,0:T(8,128)(2,1)S(1)}, bf16[64,2048]{1,0:T(8,128)(2,1)S(1)}, bf16[64,2048]{1,0:T(8,128)(2,1)S(1)}, f32[1024,128]{1,0:T(8,128)S(1)}) custom-call(bf16[64,2048]{1,0:T(8,128)(2,1)S(1)} %copy-done.6, bf16[64,2048]{1,0:T(8,128)(2,1)S(1)} %copy-done.7, bf16[64,2048]{1,0:T(8,128)(2,1)S(1)} %copy-done.8, ...), custom_call_target="tpu_custom_call" | custom-call | tf_op jit(solution)/shard_map/gated_conv_backward/pallas_call | solution.py:300
  54.1 0.7 %copy.19 = bf16[64,2048]{1,0:T(8,128)(2,1)} copy(bf16[64,2048]{1,0:T(8,128)(2,1)S(1)} %get-tuple-element.16) | data formatting | bytes 524288
  54.8 0.7 %copy.20 = bf16[64,2048]{1,0:T(8,128)(2,1)} copy(bf16[64,2048]{1,0:T(8,128)(2,1)S(1)} %get-tuple-element.17) | data formatting | bytes 524288
  55.5 0.7 %copy.21 = bf16[64,2048]{1,0:T(8,128)(2,1)} copy(bf16[64,2048]{1,0:T(8,128)(2,1)S(1)} %get-tuple-element.18) | data formatting | bytes 524288
  56.2 0.8 %copy.22 = f32[1,131072]{1,0:T(1,128)} copy(f32[1,131072]{1,0:T(1,128)S(1)} %bitcast.2) | data formatting | bytes 1048576
  (1 shorter events, 0.0 us)
Async XLA Ops:
  0.6 1.2 %copy-start = (bf16[1024,512]{1,0:T(8,128)(2,1)S(1)}, bf16[1024,512]{1,0:T(8,128)(2,1)}, u32[]{:S(2)}) copy-start(bf16[1024,512]{1,0:T(8,128)(2,1)} %constant.12.clone.first_hbm) | copy-start | bytes 3145732
  1.9 1.0 %copy-start.1 = (f32[1,131072]{1,0:T(1,128)S(1)}, f32[1,131072]{1,0:T(1,128)}, u32[]{:S(2)}) copy-start(f32[1,131072]{1,0:T(1,128)} %param.15) | copy-start | bytes 1572868
  2.9 1.0 %copy-start.2 = (f32[512,256]{1,0:T(8,128)S(1)}, f32[512,256]{1,0:T(8,128)}, u32[]{:S(2)}) copy-start(f32[512,256]{1,0:T(8,128)} %constant.17.clone.tim_hbm) | copy-start | bytes 1572868
  3.9 1.0 %copy-start.3 = (f32[512,256]{1,0:T(8,128)S(1)}, f32[512,256]{1,0:T(8,128)}, u32[]{:S(2)}) copy-start(f32[512,256]{1,0:T(8,128)} %constant.16.clone.tre_hbm) | copy-start | bytes 1572868
  5.0 1.0 %copy-start.4 = (bf16[512,512]{1,0:T(8,128)(2,1)S(1)}, bf16[512,512]{1,0:T(8,128)(2,1)}, u32[]{:S(2)}) copy-start(bf16[512,512]{1,0:T(8,128)(2,1)} %constant.15.clone.back_hbm) | copy-start | bytes 1572868
  6.0 1.0 %copy-start.5 = (bf16[512,512]{1,0:T(8,128)(2,1)S(1)}, bf16[512,512]{1,0:T(8,128)(2,1)}, u32[]{:S(2)}) copy-start(bf16[512,512]{1,0:T(8,128)(2,1)} %constant.14.clone.second_hbm) | copy-start | bytes 1572868
  7.1 0.9 %copy-start.6 = (bf16[64,2048]{1,0:T(8,128)(2,1)S(1)}, bf16[64,2048]{1,0:T(8,128)(2,1)}, u32[]{:S(2)}) copy-start(bf16[64,2048]{1,0:T(8,128)(2,1)} %q_ref.1) | copy-start | bytes 786436
  8.0 0.9 %copy-start.7 = (bf16[64,2048]{1,0:T(8,128)(2,1)S(1)}, bf16[64,2048]{1,0:T(8,128)(2,1)}, u32[]{:S(2)}) copy-start(bf16[64,2048]{1,0:T(8,128)(2,1)} %k_ref.1) | copy-start | bytes 786436
  9.0 0.9 %copy-start.8 = (bf16[64,2048]{1,0:T(8,128)(2,1)S(1)}, bf16[64,2048]{1,0:T(8,128)(2,1)}, u32[]{:S(2)}) copy-start(bf16[64,2048]{1,0:T(8,128)(2,1)} %v_ref.1) | copy-start | bytes 786436
  9.9 0.9 %copy-start.9 = (bf16[64,2048]{1,0:T(8,128)(2,1)S(1)}, bf16[64,2048]{1,0:T(8,128)(2,1)}, u32[]{:S(2)}) copy-start(bf16[64,2048]{1,0:T(8,128)(2,1)} %go_ref.1) | copy-start | bytes 786436

commit v2 on v1

--- a/solution.py
+++ b/solution.py
@@ -12,7 +12,11 @@
 LANES = 128
 ACROSS = 256
 PIECE = 2048
+ORDER = (2, 1, 3, 0)
+GROUPS = 4
 ROWS = PIECE // ACROSS
+SLICES = 4
+VMEM_GRANT = 52 * 1024 * 1024 + 512 * 1024
 
 f32 = jnp.float32
 bf16 = jnp.bfloat16
@@ -39,14 +43,15 @@
 
 def kernel(
     parts,
+    q_hbm, k_hbm, v_hbm, go_hbm, h_hbm,
+    first_hbm, last_hbm, second_hbm, back_hbm, tre_hbm, tim_hbm,
+    gq_ref, gk_ref, gv_ref, gf0_ref, gf1_ref,
     q_ref, k_ref, v_ref, go_ref, h_ref,
-    first_hbm, last_hbm, second_hbm, back_hbm, tre_hbm, tim_hbm,
-    gq_ref, gk_ref, gv_ref, gf_ref,
     first_ref, last_ref, second_ref, back_ref, tre_ref, tim_ref,
     turn_ref, msg_x, msg_g, msg_c, msg_m, got_x, got_g, got_c, got_m,
     signal_ref, mid_ref, spec_h, spec_x, spec_g,
     lag_ref, lag_in, pair_ref, pair_in, total_ref,
-    table_sem, send_sem, recv_sem, pair_send, pair_recv,
+    window_sem, load_sem, send_sem, recv_sem, pair_send, pair_recv,
 ):
     half_rows = parts * ROWS
     seq = half_rows * ACROSS
@@ -58,6 +63,15 @@
     other_high = (1 - high) * 2 + core
     MESH = pl.DeviceIdType.MESH
 
+    size = parts // GROUPS
+    plane, spot = me // size, lax.rem(me, size)
+
+    def sent_rows(i):
+        return pl.multiple_of(lax.rem(plane + ORDER[i], GROUPS) * size, size)
+
+    def got_rows(i):
+        return pl.multiple_of(lax.rem(plane + GROUPS - ORDER[i], GROUPS) * size, size)
+
     barrier = pltpu.get_barrier_semaphore()
 
     def greet(step, carry):
@@ -70,10 +84,22 @@
     pl.semaphore_signal(barrier, inc=1, device_id=(me, other_core), device_id_type=MESH)
     pl.semaphore_signal(barrier, inc=1, device_id=(me, other_high), device_id_type=MESH)
 
-    table_copies = [
-        pltpu.make_async_copy(src, dst, table_sem.at[i])
+    windows = ((k_hbm, k_ref), (v_hbm, v_ref), (go_hbm, go_ref), (q_hbm, q_ref))
+    window_loads = []
+    for pair in (windows[:2], windows[2:]):
+        for i in range(GROUPS):
+            for src, dst in pair:
+                rows = pl.ds(sent_rows(i), size)
+                load = pltpu.make_async_copy(
+                    src.at[rows], dst.at[rows], window_sem.at[len(window_loads)]
+                )
+                load.start()
+                window_loads.append(load)
+    loads = [
+        pltpu.make_async_copy(src, dst, load_sem.at[i])
         for i, (src, dst) in enumerate(
             (
+                (h_hbm, h_ref),
                 (first_hbm, first_ref),
                 (tre_hbm, tre_ref),
                 (tim_hbm, tim_ref),
@@ -83,38 +109,48 @@
             )
         )
     ]
-    for copy in table_copies:
-        copy.start()
-
-    def gate(a_ref, b_ref, msg_ref):
+    for load in loads:
+        load.start()
+
+    def gate(a_ref, b_ref, msg_ref, i):
+        start = sent_rows(i)
+        rows = pl.ds(start, size)
         for j in range(PIECE // LANES):
             cols = slice(j * LANES, (j + 1) * LANES)
             slot = (j % 2) * ROWS + j // 2
-            turn_ref[pl.ds(slot, parts, stride=16), :] = a_ref[:, cols].astype(f32) * b_ref[
-                :, cols
+            turn_ref[pl.ds(slot, size, stride=16), :] = a_ref[rows, cols].astype(f32) * b_ref[
+                rows, cols
             ].astype(f32)
-        msg_ref[...] = turn_ref[...].reshape(parts, 16, LANES).astype(bf16)
-
-    def send_all(msg_ref, got_ref, which):
+        msg_ref[rows] = turn_ref[...].reshape(size, 16, LANES).astype(bf16)
+
+    def send_group(msg_ref, got_ref, which, i):
+        start = sent_rows(i)
+
         def send(step, carry):
-            to = lax.rem(me + step, parts)
+            to = start + lax.rem(spot + step, size)
             pltpu.make_async_remote_copy(
                 src_ref=msg_ref.at[to],
                 dst_ref=got_ref.at[me],
                 send_sem=send_sem.at[which],
-                recv_sem=recv_sem.at[which],
+                recv_sem=recv_sem.at[which, i],
                 device_id=(to, group),
                 device_id_type=MESH,
             ).start()
             return carry
 
-        lax.fori_loop(1, parts, send, 0)
-        got_ref[me] = msg_ref[me]
-
-    def whole(ref, sem):
-        return pltpu.make_async_copy(
-            ref.at[pl.ds(0, parts - 1)], ref.at[pl.ds(0, parts - 1)], sem
-        )
+        lax.fori_loop(1 if ORDER[i] == 0 else 0, size, send, 0)
+        if ORDER[i] == 0:
+            got_ref[me] = msg_ref[me]
+
+    def wait_group(got_ref, which, i):
+        count = size - 1 if ORDER[i] == 0 else size
+        if count:
+            some = got_ref.at[pl.ds(0, count)]
+            pltpu.make_async_copy(some, some, recv_sem.at[which, i]).wait()
+
+    def wait_all(got_ref, which):
+        for i in range(GROUPS):
+            wait_group(got_ref, which, i)
 
     def unfold(got_ref):
         got = got_ref[...].astype(f32)
@@ -163,60 +199,64 @@
 
         lax.fori_loop(0, 2, body, 0)
 
-    def inverse_rows(c, scale):
-        rows = pl.ds(pl.multiple_of(c * chunk, chunk), chunk)
-        return (
-            jnp.dot(last_ref[rows, :], mid_ref[...], preferred_element_type=f32) * scale
-        )
-
-    def inverse_to_msg(a_spec, b_spec, conj, msg_ref):
-        inverse_mid(a_spec, b_spec, conj)
-
-        def body(c, carry):
-            out = inverse_rows(c, 1.0 / seq)
+    def inverse_rows_and_send(msg_ref, got_ref, which):
+        for i in range(GROUPS):
+            start = sent_rows(i)
+            rows = pl.ds(pl.multiple_of(start * ROWS, size * ROWS), size * ROWS)
+            out = jnp.dot(last_ref[rows, :], mid_ref[...], preferred_element_type=f32) * (1.0 / seq)
             out = jnp.concatenate(
                 [
-                    out[:, :LANES].reshape(parts // 2, ROWS, LANES),
-                    out[:, LANES:].reshape(parts // 2, ROWS, LANES),
+                    out[:, :LANES].reshape(size, ROWS, LANES),
+                    out[:, LANES:].reshape(size, ROWS, LANES),
                 ],
                 1,
             )
-            msg_ref[pl.ds(c * (parts // 2), parts // 2)] = out.astype(bf16)
-            return carry
-
-        lax.fori_loop(0, 2, body, 0)
-
-    gate(k_ref, v_ref, msg_x)
-    pl.semaphore_wait(barrier, parts + 1)
-    send_all(msg_x, got_x, 0)
-    gate(go_ref, q_ref, msg_g)
-    send_all(msg_g, got_g, 1)
+            msg_ref[pl.ds(start, size)] = out.astype(bf16)
+            send_group(msg_ref, got_ref, which, i)
+
+    for i in range(GROUPS):
+        window_loads[2 * i].wait()
+        window_loads[2 * i + 1].wait()
+        gate(k_ref, v_ref, msg_x, i)
+        if i == 0:
+            pl.semaphore_wait(barrier, parts + 1)
+        send_group(msg_x, got_x, 0, i)
+    for i in range(GROUPS):
+        window_loads[2 * (GROUPS + i)].wait()
+        window_loads[2 * (GROUPS + i) + 1].wait()
+        gate(go_ref, q_ref, msg_g, i)
+        send_group(msg_g, got_g, 1, i)
 
     root = math.sqrt(seq)
+    loads[0].wait()
     for half in range(2):
         signal_ref[:, half * LANES : (half + 1) * LANES] = (
             h_ref[pl.ds(half, half_rows, stride=2), :] * (1.0 / root)
         ).astype(bf16)
-    for copy in table_copies[:4]:
-        copy.wait()
+    for load in loads[1:5]:
+        load.wait()
     forward(spec_h)
 
-    whole(got_x, recv_sem.at[0]).wait()
+    wait_all(got_x, 0)
     unfold(got_x)
     forward(spec_x)
-    for copy in table_copies[4:]:
-        copy.wait()
-    inverse_to_msg(spec_h, spec_x, False, msg_c)
-    send_all(msg_c, got_c, 2)
-
-    whole(got_g, recv_sem.at[1]).wait()
+    for load in loads[5:]:
+        load.wait()
+    inverse_mid(spec_h, spec_x, False)
+    inverse_rows_and_send(msg_c, got_c, 2)
+
+    wait_all(got_g, 1)
     unfold(got_g)
     forward(spec_g)
 
     inverse_mid(spec_x, spec_g, True)
 
     def lag_body(c, carry):
-        lag_ref[c] = inverse_rows(c, 1.0 / (seq * root)).astype(bf16)
+        rows = pl.ds(pl.multiple_of(c * chunk, chunk), chunk)
+        lag_ref[c] = (
+            jnp.dot(last_ref[rows, :], mid_ref[...], preferred_element_type=f32)
+            * (1.0 / (seq * root))
+        ).astype(bf16)
         return carry
 
     lax.fori_loop(0, 2, lag_body, 0)
@@ -231,7 +271,7 @@
     )
     to_core.start()
 
-    inverse_to_msg(spec_h, spec_g, True, msg_m)
+    inverse_mid(spec_h, spec_g, True)
     to_core.wait_recv()
     pair_ref[...] = (lag_ref[core].astype(f32) + lag_in[...].astype(f32)).astype(bf16)
     to_high = pltpu.make_async_remote_copy(
@@ -243,15 +283,21 @@
         device_id_type=MESH,
     )
     to_high.start()
-    send_all(msg_m, got_m, 3)
-
-    whole(got_c, recv_sem.at[2]).wait()
-    turn_ref[...] = got_c[...].astype(f32).reshape(parts * 16, LANES)
-    for j in range(PIECE // LANES):
-        cols = slice(j * LANES, (j + 1) * LANES)
-        slot = (j % 2) * ROWS + j // 2
-        conv = turn_ref[pl.ds(slot, parts, stride=16), :]
-        gq_ref[:, cols] = (go_ref[:, cols].astype(f32) * conv).astype(bf16)
+    inverse_rows_and_send(msg_m, got_m, 3)
+
+    def finish(got_ref, which, i, terms):
+        wait_group(got_ref, which, i)
+        rows = pl.ds(got_rows(i), size)
+        turn_ref[...] = got_ref[rows].astype(f32).reshape(size * 16, LANES)
+        for j in range(PIECE // LANES):
+            cols = slice(j * LANES, (j + 1) * LANES)
+            slot = (j % 2) * ROWS + j // 2
+            value = turn_ref[pl.ds(slot, size, stride=16), :]
+            for factor_ref, out_ref in terms:
+                out_ref[rows, cols] = (factor_ref[rows, cols].astype(f32) * value).astype(bf16)
+
+    for i in range(GROUPS):
+        finish(got_c, 2, i, ((go_ref, gq_ref),))
 
     to_high.wait_recv()
     total_ref[core] = pair_ref[...].astype(f32) + pair_in[...].astype(f32)
@@ -265,26 +311,43 @@
     )
     to_core_again.start()
 
-    whole(got_m, recv_sem.at[3]).wait()
-    turn_ref[...] = got_m[...].astype(f32).reshape(parts * 16, LANES)
-    for j in range(PIECE // LANES):
-        cols = slice(j * LANES, (j + 1) * LANES)
-        slot = (j % 2) * ROWS + j // 2
-        mixed = turn_ref[pl.ds(slot, parts, stride=16), :]
-        gk_ref[:, cols] = (mixed * v_ref[:, cols].astype(f32)).astype(bf16)
-        gv_ref[:, cols] = (mixed * k_ref[:, cols].astype(f32)).astype(bf16)
-
     to_core_again.wait_recv()
-    for c in range(2):
+    for c, gf_ref in enumerate((gf0_ref, gf1_ref)):
         for half in range(2):
-            gf_ref[pl.ds(c * half_rows + half, chunk, stride=2), :] = total_ref[
+            gf_ref[pl.ds(half, chunk, stride=2), :] = total_ref[
                 c, :, half * LANES : (half + 1) * LANES
             ]
+
+    for i in range(GROUPS):
+        finish(got_m, 3, i, ((v_ref, gk_ref), (k_ref, gv_ref)))
+
     for which, ref in enumerate((msg_x, msg_g, msg_c, msg_m)):
-        whole(ref, send_sem.at[which]).wait()
+        some = ref.at[pl.ds(0, parts - 1)]
+        pltpu.make_async_copy(some, some, send_sem.at[which]).wait()
     to_core.wait_send()
     to_high.wait_send()
     to_core_again.wait_send()
+
+
+def write_out(*refs):
+    sources, targets, sem = refs[:5], refs[5:9], refs[9]
+    copies = []
+    for i, source in enumerate(sources):
+        height = source.shape[0]
+        step = height // SLICES
+        target, base = (targets[i], 0) if i < 3 else (targets[3], (i - 3) * height)
+        for part in range(SLICES):
+            copies.append(
+                pltpu.make_async_copy(
+                    source.at[pl.ds(part * step, step)],
+                    target.at[pl.ds(base + part * step, step)],
+                    sem.at[len(copies)],
+                )
+            )
+    for copy in copies:
+        copy.start()
+    for copy in copies:
+        copy.wait()
 
 
 def per_device(parts, query_in, key_in, value_in, grad_out, filter_raw):
@@ -292,18 +355,21 @@
     seq = half_rows * ACROSS
     tables = make_tables(half_rows)
     vmem = pl.BlockSpec(memory_space=pltpu.VMEM)
-    anywhere = pl.BlockSpec(memory_space=pl.ANY)
+    hbm = pl.BlockSpec(memory_space=pltpu.HBM)
     window = jax.ShapeDtypeStruct((parts, PIECE), bf16)
+    taps = jax.ShapeDtypeStruct((seq // (2 * LANES), LANES), f32)
     message = pltpu.VMEM((parts, 16, LANES), bf16)
     spectrum = pltpu.VMEM((half_rows, 2 * ACROSS), f32)
     half = (half_rows // 2, ACROSS)
     outs = pl.pallas_call(
         functools.partial(kernel, parts),
-        out_shape=(window, window, window, jax.ShapeDtypeStruct((seq // LANES, LANES), f32)),
-        in_specs=[vmem] * 5 + [anywhere] * 6,
-        out_specs=(vmem, vmem, vmem, vmem),
-        scratch_shapes=[pltpu.VMEM(t.shape, t.dtype) for t in tables]
-        + [pltpu.VMEM((parts * 16, LANES), f32)]
+        out_shape=(window, window, window, taps, taps),
+        in_specs=[hbm] * 11,
+        out_specs=(vmem,) * 5,
+        scratch_shapes=[pltpu.VMEM((parts, PIECE), bf16)] * 4
+        + [pltpu.VMEM((seq // LANES, LANES), f32)]
+        + [pltpu.VMEM(t.shape, t.dtype) for t in tables]
+        + [pltpu.VMEM((parts // GROUPS * 16, LANES), f32)]
         + [message] * 8
         + [
             pltpu.VMEM((half_rows, ACROSS), bf16),
@@ -316,14 +382,15 @@
             pltpu.VMEM(half, bf16),
             pltpu.VMEM(half, bf16),
             pltpu.VMEM((2,) + half, f32),
-            pltpu.SemaphoreType.DMA((6,)),
+            pltpu.SemaphoreType.DMA((4 * GROUPS,)),
+            pltpu.SemaphoreType.DMA((7,)),
             pltpu.SemaphoreType.DMA((4,)),
-            pltpu.SemaphoreType.DMA((4,)),
+            pltpu.SemaphoreType.DMA((4, GROUPS)),
             pltpu.SemaphoreType.DMA((3,)),
             pltpu.SemaphoreType.DMA((3,)),
         ],
         compiler_params=pltpu.CompilerParams(
-            collective_id=0, has_side_effects=True, vmem_limit_bytes=48 * 1024 * 1024
+            collective_id=0, has_side_effects=True, vmem_limit_bytes=VMEM_GRANT
         ),
         name="gated_conv_backward",
     )(
@@ -334,6 +401,15 @@
         filter_raw.reshape(seq // LANES, LANES),
         *(jnp.asarray(t) for t in tables),
     )
+    outs = pl.pallas_call(
+        write_out,
+        out_shape=(window, window, window, jax.ShapeDtypeStruct((seq // LANES, LANES), f32)),
+        in_specs=[pl.BlockSpec(memory_space=pl.ANY)] * 5,
+        out_specs=[hbm] * 4,
+        scratch_shapes=[pltpu.SemaphoreType.DMA((5 * SLICES,))],
+        compiler_params=pltpu.CompilerParams(vmem_limit_bytes=VMEM_GRANT),
+        name="write_out",
+    )(*outs)
     return (outs[0], outs[1], outs[2], outs[3].reshape(1, seq))
 
 

time: 58.1 us -> 46.5 us (0.80); the launches traced: 57 us -> 46.4 us
  local copies, waits for them, and re-layouts: 13.1 us -> 0 us
  Pallas kernels: 43.2 us -> 45.7 us
    unnamed x24 -> x0, local copies, waits for them, and re-layouts: 13.1 us -> none
    pallas_call x1, Pallas kernels: 43.2 us -> 44.5 us  [per_device(): pl.pallas_call(functools.partial(kernel, parts), out_shape=(window, windo...]
    pallas_call x0 -> x1, Pallas kernels: none -> 1.21 us  [per_device(): pl.pallas_call(write_out, out_shape=(window, window, window, jax.ShapeDty...]
where the time goes in v2:
time: 46.5 us; the launch traced here: 46.4 us
  Pallas kernels  45.7 us (98%)
  between operations  0.64 us (1%)
    pallas_call x1, Pallas kernels, per_device(): pl.pallas_call(functools.partial(kernel, parts), out_shape=(window, windo...  44.5 us
    pallas_call x1, Pallas kernels, per_device(): pl.pallas_call(write_out, out_shape=(window, window, window, jax.ShapeDty...  1.21 us

profile of v2, /device:TPU:1, one launch (start us, length us, event | category | flops | bytes accessed | tf_op | source)
XLA Modules:
  0.0 46.4 jit_solution(91199398657917426)
XLA Ops:
  0.6 44.5 %gated_conv_backward.1 = (bf16[64,2048]{1,0:T(8,128)(2,1)S(1)}, bf16[64,2048]{1,0:T(8,128)(2,1)S(1)}, bf16[64,2048]{1,0:T(8,128)(2,1)S(1)}, f32[512,128]{1,0:T(8,128)S(1)}, f32[512,128]{1,0:T(8,128)S(1)}) custom-call(bf16[64,2048]{1,0:T(8,128)(2,1)} %q_hbm.1, bf16[64,2048]{1,0:T(8,128)(2,1)} %k_hbm.1, bf16[64,2048]{1,0:T(8,128)(2,1)} %v_hbm.1, ...), custom_call_target="tpu_custom_call" | custom-call | tf_op jit(solution)/shard_map/gated_conv_backward/pallas_call | solution.py:364
  45.2 1.2 %write_out.1 = (bf16[64,2048]{1,0:T(8,128)(2,1)}, bf16[64,2048]{1,0:T(8,128)(2,1)}, bf16[64,2048]{1,0:T(8,128)(2,1)}, f32[1024,128]{1,0:T(8,128)}) custom-call(bf16[64,2048]{1,0:T(8,128)(2,1)S(1)} %get-tuple-element.13.refs_0_, bf16[64,2048]{1,0:T(8,128)(2,1)S(1)} %get-tuple-element.14.refs_1_, bf16[64,2048]{1,0:T(8,128)(2,1)S(1)} %get-tuple-element.15.refs_2_, ...), custom_call_target="tpu_custom_call" | custom-call | tf_op jit(solution)/shard_map/write_out/pallas_call | solution.py:404

commit v3 on v2

--- a/solution.py
+++ b/solution.py
@@ -52,6 +52,7 @@
     signal_ref, mid_ref, spec_h, spec_x, spec_g,
     lag_ref, lag_in, pair_ref, pair_in, total_ref,
     window_sem, load_sem, send_sem, recv_sem, pair_send, pair_recv,
+    high_send, high_recv, share_send, share_recv,
 ):
     half_rows = parts * ROWS
     seq = half_rows * ACROSS
@@ -249,6 +250,8 @@
     unfold(got_g)
     forward(spec_g)
 
+    inverse_mid(spec_h, spec_g, True)
+    inverse_rows_and_send(msg_m, got_m, 3)
     inverse_mid(spec_x, spec_g, True)
 
     def lag_body(c, carry):
@@ -271,19 +274,22 @@
     )
     to_core.start()
 
-    inverse_mid(spec_h, spec_g, True)
     to_core.wait_recv()
     pair_ref[...] = (lag_ref[core].astype(f32) + lag_in[...].astype(f32)).astype(bf16)
-    to_high = pltpu.make_async_remote_copy(
-        src_ref=pair_ref,
-        dst_ref=pair_in,
-        send_sem=pair_send.at[1],
-        recv_sem=pair_recv.at[1],
-        device_id=(me, other_high),
-        device_id_type=MESH,
-    )
-    to_high.start()
-    inverse_rows_and_send(msg_m, got_m, 3)
+    quarter = half_rows // 8
+    to_high = [
+        pltpu.make_async_remote_copy(
+            src_ref=pair_ref.at[pl.ds(n * quarter, quarter)],
+            dst_ref=pair_in.at[pl.ds(n * quarter, quarter)],
+            send_sem=high_send.at[n],
+            recv_sem=high_recv.at[n],
+            device_id=(me, other_high),
+            device_id_type=MESH,
+        )
+        for n in range(4)
+    ]
+    for copy in to_high:
+        copy.start()
 
     def finish(got_ref, which, i, terms):
         wait_group(got_ref, which, i)
@@ -299,34 +305,38 @@
     for i in range(GROUPS):
         finish(got_c, 2, i, ((go_ref, gq_ref),))
 
-    to_high.wait_recv()
-    total_ref[core] = pair_ref[...].astype(f32) + pair_in[...].astype(f32)
-    to_core_again = pltpu.make_async_remote_copy(
-        src_ref=total_ref.at[core],
-        dst_ref=total_ref.at[core],
-        send_sem=pair_send.at[2],
-        recv_sem=pair_recv.at[2],
-        device_id=(me, other_core),
-        device_id_type=MESH,
-    )
-    to_core_again.start()
-
-    to_core_again.wait_recv()
+    for i in (0, 1, 2, 3):
+        finish(got_m, 3, i, ((v_ref, gk_ref), (k_ref, gv_ref)))
+
+    to_core_again = []
+    for n in range(4):
+        rows = pl.ds(n * quarter, quarter)
+        to_high[n].wait_recv()
+        total_ref[core, rows] = pair_ref[rows].astype(f32) + pair_in[rows].astype(f32)
+        copy = pltpu.make_async_remote_copy(
+            src_ref=total_ref.at[core, rows],
+            dst_ref=total_ref.at[core, rows],
+            send_sem=share_send.at[n],
+            recv_sem=share_recv.at[n],
+            device_id=(me, other_core),
+            device_id_type=MESH,
+        )
+        copy.start()
+        to_core_again.append(copy)
+    for copy in to_core_again:
+        copy.wait_recv()
     for c, gf_ref in enumerate((gf0_ref, gf1_ref)):
         for half in range(2):
             gf_ref[pl.ds(half, chunk, stride=2), :] = total_ref[
                 c, :, half * LANES : (half + 1) * LANES
             ]
 
-    for i in range(GROUPS):
-        finish(got_m, 3, i, ((v_ref, gk_ref), (k_ref, gv_ref)))
-
     for which, ref in enumerate((msg_x, msg_g, msg_c, msg_m)):
         some = ref.at[pl.ds(0, parts - 1)]
         pltpu.make_async_copy(some, some, send_sem.at[which]).wait()
     to_core.wait_send()
-    to_high.wait_send()
-    to_core_again.wait_send()
+    for copy in to_high + to_core_again:
+        copy.wait_send()
 
 
 def write_out(*refs):
@@ -386,8 +396,12 @@
             pltpu.SemaphoreType.DMA((7,)),
             pltpu.SemaphoreType.DMA((4,)),
             pltpu.SemaphoreType.DMA((4, GROUPS)),
-            pltpu.SemaphoreType.DMA((3,)),
-            pltpu.SemaphoreType.DMA((3,)),
+            pltpu.SemaphoreType.DMA((1,)),
+            pltpu.SemaphoreType.DMA((1,)),
+            pltpu.SemaphoreType.DMA((4,)),
+            pltpu.SemaphoreType.DMA((4,)),
+            pltpu.SemaphoreType.DMA((4,)),
+            pltpu.SemaphoreType.DMA((4,)),
         ],
         compiler_params=pltpu.CompilerParams(
             collective_id=0, has_side_effects=True, vmem_limit_bytes=VMEM_GRANT

time: 46.5 us -> 45.9 us (0.987)
  the two profiles are of different devices: /device:TPU:1 before, /device:TPU:33 now
where the time goes in v3:
time: 45.9 us; the launch traced here: 45.8 us
  Pallas kernels  45.2 us (98%)
  between operations  0.64 us (1%)
    pallas_call x1, Pallas kernels, per_device(): pl.pallas_call(functools.partial(kernel, parts), out_shape=(window, windo...  44 us
    pallas_call x1, Pallas kernels, per_device(): pl.pallas_call(write_out, out_shape=(window, window, window, jax.ShapeDty...  1.21 us

profile of v3, /device:TPU:33, one launch (start us, length us, event | category | flops | bytes accessed | tf_op | source)
XLA Modules:
  0.0 45.8 jit_solution(18043464890061735868)
XLA Ops:
  0.6 44.0 %gated_conv_backward.1 = (bf16[64,2048]{1,0:T(8,128)(2,1)S(1)}, bf16[64,2048]{1,0:T(8,128)(2,1)S(1)}, bf16[64,2048]{1,0:T(8,128)(2,1)S(1)}, f32[512,128]{1,0:T(8,128)S(1)}, f32[512,128]{1,0:T(8,128)S(1)}) custom-call(bf16[64,2048]{1,0:T(8,128)(2,1)} %q_hbm.1, bf16[64,2048]{1,0:T(8,128)(2,1)} %k_hbm.1, bf16[64,2048]{1,0:T(8,128)(2,1)} %v_hbm.1, ...), custom_call_target="tpu_custom_call" | custom-call | tf_op jit(solution)/shard_map/gated_conv_backward/pallas_call | solution.py:374
  44.6 1.2 %write_out.1 = (bf16[64,2048]{1,0:T(8,128)(2,1)}, bf16[64,2048]{1,0:T(8,128)(2,1)}, bf16[64,2048]{1,0:T(8,128)(2,1)}, f32[1024,128]{1,0:T(8,128)}) custom-call(bf16[64,2048]{1,0:T(8,128)(2,1)S(1)} %get-tuple-element.13.refs_0_, bf16[64,2048]{1,0:T(8,128)(2,1)S(1)} %get-tuple-element.14.refs_1_, bf16[64,2048]{1,0:T(8,128)(2,1)S(1)} %get-tuple-element.15.refs_2_, ...), custom_call_target="tpu_custom_call" | custom-call | tf_op jit(solution)/shard_map/write_out/pallas_call | solution.py:418

commit v4 on v3

--- a/solution.py
+++ b/solution.py
@@ -254,16 +254,14 @@
     inverse_rows_and_send(msg_m, got_m, 3)
     inverse_mid(spec_x, spec_g, True)
 
-    def lag_body(c, carry):
+    def lag_half(c):
         rows = pl.ds(pl.multiple_of(c * chunk, chunk), chunk)
         lag_ref[c] = (
             jnp.dot(last_ref[rows, :], mid_ref[...], preferred_element_type=f32)
             * (1.0 / (seq * root))
         ).astype(bf16)
-        return carry
-
-    lax.fori_loop(0, 2, lag_body, 0)
-
+
+    lag_half(1 - core)
     to_core = pltpu.make_async_remote_copy(
         src_ref=lag_ref.at[1 - core],
         dst_ref=lag_in,
@@ -273,9 +271,9 @@
         device_id_type=MESH,
     )
     to_core.start()
+    lag_half(core)
 
     to_core.wait_recv()
-    pair_ref[...] = (lag_ref[core].astype(f32) + lag_in[...].astype(f32)).astype(bf16)
     quarter = half_rows // 8
     to_high = [
         pltpu.make_async_remote_copy(
@@ -288,8 +286,10 @@
         )
         for n in range(4)
     ]
-    for copy in to_high:
-        copy.start()
+    for n in range(4):
+        rows = pl.ds(n * quarter, quarter)
+        pair_ref[rows] = (lag_ref[core, rows].astype(f32) + lag_in[rows].astype(f32)).astype(bf16)
+        to_high[n].start()
 
     def finish(got_ref, which, i, terms):
         wait_group(got_ref, which, i)

time: 45.9 us -> 46.2 us (level)
  the two profiles are of different devices: /device:TPU:33 before, /device:TPU:1 now
where the time goes in v4:
time: 46.2 us; the launch traced here: 45.3 us
  Pallas kernels  44.7 us (97%)
  between operations  0.64 us (1%)
    pallas_call x1, Pallas kernels, per_device(): pl.pallas_call(functools.partial(kernel, parts), out_shape=(window, windo...  43.5 us
    pallas_call x1, Pallas kernels, per_device(): pl.pallas_call(write_out, out_shape=(window, window, window, jax.ShapeDty...  1.21 us

profile of v4, /device:TPU:1, one launch (start us, length us, event | category | flops | bytes accessed | tf_op | source)
XLA Modules:
  0.0 45.3 jit_solution(1834582745252708388)
XLA Ops:
  0.6 43.5 %gated_conv_backward.1 = (bf16[64,2048]{1,0:T(8,128)(2,1)S(1)}, bf16[64,2048]{1,0:T(8,128)(2,1)S(1)}, bf16[64,2048]{1,0:T(8,128)(2,1)S(1)}, f32[512,128]{1,0:T(8,128)S(1)}, f32[512,128]{1,0:T(8,128)S(1)}) custom-call(bf16[64,2048]{1,0:T(8,128)(2,1)} %q_hbm.1, bf16[64,2048]{1,0:T(8,128)(2,1)} %k_hbm.1, bf16[64,2048]{1,0:T(8,128)(2,1)} %v_hbm.1, ...), custom_call_target="tpu_custom_call" | custom-call | tf_op jit(solution)/shard_map/gated_conv_backward/pallas_call | solution.py:374
  44.1 1.2 %write_out.1 = (bf16[64,2048]{1,0:T(8,128)(2,1)}, bf16[64,2048]{1,0:T(8,128)(2,1)}, bf16[64,2048]{1,0:T(8,128)(2,1)}, f32[1024,128]{1,0:T(8,128)}) custom-call(bf16[64,2048]{1,0:T(8,128)(2,1)S(1)} %get-tuple-element.13.refs_0_, bf16[64,2048]{1,0:T(8,128)(2,1)S(1)} %get-tuple-element.14.refs_1_, bf16[64,2048]{1,0:T(8,128)(2,1)S(1)} %get-tuple-element.15.refs_2_, ...), custom_call_target="tpu_custom_call" | custom-call | tf_op jit(solution)/shard_map/write_out/pallas_call | solution.py:418

commit v5 on v3

--- a/solution.py
+++ b/solution.py
@@ -67,8 +67,13 @@
     size = parts // GROUPS
     plane, spot = me // size, lax.rem(me, size)
 
+    odd = lax.rem(spot, 2)
+
+    def distance(i):
+        return (2, 1 + 2 * odd, 3 - 2 * odd, 0)[i]
+
     def sent_rows(i):
-        return pl.multiple_of(lax.rem(plane + ORDER[i], GROUPS) * size, size)
+        return pl.multiple_of(lax.rem(plane + distance(i), GROUPS) * size, size)
 
     def got_rows(i):
         return pl.multiple_of(lax.rem(plane + GROUPS - ORDER[i], GROUPS) * size, size)
@@ -133,7 +138,7 @@
                 src_ref=msg_ref.at[to],
                 dst_ref=got_ref.at[me],
                 send_sem=send_sem.at[which],
-                recv_sem=recv_sem.at[which, i],
+                recv_sem=recv_sem.at[which, distance(i)],
                 device_id=(to, group),
                 device_id_type=MESH,
             ).start()
@@ -147,7 +152,7 @@
         count = size - 1 if ORDER[i] == 0 else size
         if count:
             some = got_ref.at[pl.ds(0, count)]
-            pltpu.make_async_copy(some, some, recv_sem.at[which, i]).wait()
+            pltpu.make_async_copy(some, some, recv_sem.at[which, ORDER[i]]).wait()
 
     def wait_all(got_ref, which):
         for i in range(GROUPS):

time: 45.9 us -> 45.9 us (level)
  the two profiles are of different devices: /device:TPU:33 before, /device:TPU:1 now
where the time goes in v5:
time: 45.9 us; the launch traced here: 45 us
  Pallas kernels  44.4 us (97%)
  between operations  0.64 us (1%)
    pallas_call x1, Pallas kernels, per_device(): pl.pallas_call(functools.partial(kernel, parts), out_shape=(window, windo...  43.2 us
    pallas_call x1, Pallas kernels, per_device(): pl.pallas_call(write_out, out_shape=(window, window, window, jax.ShapeDty...  1.21 us

profile of v5, /device:TPU:1, one launch (start us, length us, event | category | flops | bytes accessed | tf_op | source)
XLA Modules:
  0.0 45.0 jit_solution(16399549074380394933)
XLA Ops:
  0.6 43.2 %gated_conv_backward.1 = (bf16[64,2048]{1,0:T(8,128)(2,1)S(1)}, bf16[64,2048]{1,0:T(8,128)(2,1)S(1)}, bf16[64,2048]{1,0:T(8,128)(2,1)S(1)}, f32[512,128]{1,0:T(8,128)S(1)}, f32[512,128]{1,0:T(8,128)S(1)}) custom-call(bf16[64,2048]{1,0:T(8,128)(2,1)} %q_hbm.1, bf16[64,2048]{1,0:T(8,128)(2,1)} %k_hbm.1, bf16[64,2048]{1,0:T(8,128)(2,1)} %v_hbm.1, ...), custom_call_target="tpu_custom_call" | custom-call | tf_op jit(solution)/shard_map/gated_conv_backward/pallas_call | solution.py:379
  43.8 1.2 %write_out.1 = (bf16[64,2048]{1,0:T(8,128)(2,1)}, bf16[64,2048]{1,0:T(8,128)(2,1)}, bf16[64,2048]{1,0:T(8,128)(2,1)}, f32[1024,128]{1,0:T(8,128)}) custom-call(bf16[64,2048]{1,0:T(8,128)(2,1)S(1)} %get-tuple-element.13.refs_0_, bf16[64,2048]{1,0:T(8,128)(2,1)S(1)} %get-tuple-element.14.refs_1_, bf16[64,2048]{1,0:T(8,128)(2,1)S(1)} %get-tuple-element.15.refs_2_, ...), custom_call_target="tpu_custom_call" | custom-call | tf_op jit(solution)/shard_map/write_out/pallas_call | solution.py:423
